TPU v7x, 32 devices: a whole 2x2x4 slice. The times are simulated.
32 devices in a mesh: runs: 2 (over x), patch: 8 (over z, y), sub: 2 (over core).
Axes of the slice: x: 2, y: 2, z: 4, core: 2. Of those that a mesh axis runs over, the one named last changes fastest.
Arguments:
- eta_c: float32 [6144, 768], P(('runs', 'patch', 'sub')), parts along dimension 0, may hold values from -4 to 4
- u_c: float32 [6144, 768], P(('runs', 'patch', 'sub')), parts along dimension 0, may hold values from -4 to 4
- v_c: float32 [6144, 768], P(('runs', 'patch', 'sub')), parts along dimension 0, may hold values from -4 to 4
- depth_c: float32 [6144, 768], P(('runs', 'patch', 'sub')), parts along dimension 0, may hold values from 0.2 to 1
- eta_f: float32 [12288, 512], P(('runs', 'patch', 'sub')), parts along dimension 0, may hold values from -4 to 4
- u_f: float32 [12288, 512], P(('runs', 'patch', 'sub')), parts along dimension 0, may hold values from -4 to 4
- v_f: float32 [12288, 512], P(('runs', 'patch', 'sub')), parts along dimension 0, may hold values from -4 to 4
- wet_f: int32 [12288, 512], P(('runs', 'patch', 'sub')), parts along dimension 0, may hold values 0 or 1
- topography: float32 [3072, 2, 512], P(('runs', 'patch', 'sub')), parts along dimension 0, may hold values from 0.2 to 1
- owner_list: int32 [6144, 1], P('runs'), parts along dimension 0, may hold values from 0 to 7; in each aligned block of 192 rows (0 to 191, 192 to 383, ...) at most 48 rows name the same one
- block_list: int32 [6144], P('runs'), parts along dimension 0, may hold values from 0 to 95
- fault_row: float32 [512], P(('runs', 'patch', 'sub')), parts along dimension 0, may hold values from 0 to 3072
- fault_col: float32 [512], P(('runs', 'patch', 'sub')), parts along dimension 0, may hold values from 0 to 768
- fault_width: float32 [512], P(('runs', 'patch', 'sub')), parts along dimension 0, may hold values from 3 to 12
- fault_slip: float32 [512], P(('runs', 'patch', 'sub')), parts along dimension 0, may hold values from -5 to 5
Outputs:
- eta_c_out: float32 [6144, 768], P(('runs', 'patch', 'sub')), parts along dimension 0
- u_c_out: float32 [6144, 768], P(('runs', 'patch', 'sub')), parts along dimension 0
- v_c_out: float32 [6144, 768], P(('runs', 'patch', 'sub')), parts along dimension 0
- eta_f_out: float32 [12288, 512], P(('runs', 'patch', 'sub')), parts along dimension 0
- u_f_out: float32 [12288, 512], P(('runs', 'patch', 'sub')), parts along dimension 0
- v_f_out: float32 [12288, 512], P(('runs', 'patch', 'sub')), parts along dimension 0
There are 2 independent parts, one for each index of `runs`. A program takes and returns all parts, laid end to end along the dimension named above; each array names one. Nothing has to cross between parts.
Inputs may be any that keep to these rules, and one draw needn't show every extreme that they name: `owner_list`: within each device's 192 fine blocks no owner is named more than 48 times, a bound that some block reaches.
All inputs are finite; a program needn't handle non-finite values. No bound on the sum of `wet_f` on one device may be relied on, other than what follows from the above.
Results may differ from a plain program's by a relative error of at most 0.0003.
Values sent between devices are 32-bit elements; how exact they have to be, the bound alone decides.
A program may use at most 64 MiB of HBM per device.

v0:
```python
import jax
import jax.numpy as jnp
from jax import lax
from jax.sharding import PartitionSpec as P

FP = 2


courant = 0.35


def shifted(block, axis, distance):
    devices = range(lax.axis_size(axis))
    route = [(i - distance, i) for i in devices if i - distance in devices]
    return lax.ppermute(block, axis, route)


def west_faces(eta, u, depth, wet, ghost, west_open):
    rows = eta.shape[0]
    zero_col = jnp.zeros((rows, 1), jnp.float32)
    eta_west = jnp.concatenate([ghost[:, None], eta[:, :-1]], 1)
    h_west = jnp.concatenate([depth[:, :1], 0.5 * (depth[:, :-1] + depth[:, 1:])], 1)
    m_west = jnp.concatenate([wet[:, :1] * west_open, wet[:, :-1] * wet[:, 1:]], 1)
    u_new = (u - courant * (eta - eta_west)) * m_west
    flux_x = h_west * u_new
    flux_east = jnp.concatenate([flux_x[:, 1:], zero_col], 1)
    return (u_new, flux_east - flux_x)


def south_faces(eta, v, depth, wet, eta_low, h_low, m_low):
    eta_south = jnp.concatenate([eta_low, eta[:-1]], 0)
    h_south = jnp.concatenate([h_low, depth[:-1]], 0)
    m_south = jnp.concatenate([m_low, wet[:-1]], 0)
    v_new = (v - courant * (eta - eta_south)) * wet * m_south
    flux_y = 0.5 * (depth + h_south) * v_new
    return (v_new, flux_y)


def rims(depth, wet):
    return shifted(jnp.concatenate([depth[-1:], wet[-1:]], 0), ("patch", "sub"), 1)


def advance(eta, u, v, depth, wet, statics, ghost, west_open):
    eta_low = shifted(eta[-1:], ("patch", "sub"), 1)
    v_new, flux_y = south_faces(eta, v, depth, wet, eta_low, statics[:1], statics[1:])
    flux_upper = shifted(flux_y[:1], ("patch", "sub"), -1)
    flux_north = jnp.concatenate([flux_y[1:], flux_upper], 0)
    u_new, spread_x = west_faces(eta, u, depth, wet, ghost, west_open)
    eta_new = eta - courant * (spread_x + flux_north - flux_y)
    return (eta_new, u_new, v_new)


def on_device(
    eta_c,
    u_c,
    v_c,
    depth_c,
    eta_f,
    u_f,
    v_f,
    wet_f,
    topography,
    owner_list,
    block_list,
    fault_row,
    fault_col,
    fault_width,
    fault_slip,
):
    rows_c, cols_c = eta_c.shape
    rows_f, cols_f = eta_f.shape
    n_patch = lax.axis_size("patch")
    n_sub = lax.axis_size("sub")
    count = rows_f // FP
    capacity = max(2, 2 * count // n_patch)
    device = lax.axis_index(("patch", "sub"))
    me_patch = lax.axis_index("patch")
    me_sub = lax.axis_index("sub")
    first_row = (device * rows_c).astype(jnp.float32)
    rows_idx = first_row + jnp.arange(rows_c, dtype=jnp.float32)
    cols_idx = jnp.arange(cols_c, dtype=jnp.float32)
    centre_row = lax.all_gather(fault_row, ("patch", "sub"), axis=0, tiled=True)
    centre_col = lax.all_gather(fault_col, ("patch", "sub"), axis=0, tiled=True)
    widths = lax.all_gather(fault_width, ("patch", "sub"), axis=0, tiled=True)
    slips = lax.all_gather(fault_slip, ("patch", "sub"), axis=0, tiled=True)
    along_y = (rows_idx[:, None] - centre_row[None, :]) / widths[None, :]
    along = jnp.exp(-along_y * along_y) * slips[None, :]
    across_x = (cols_idx[None, :] - centre_col[:, None]) / widths[:, None]
    across = (1.0 + across_x) * jnp.exp(-across_x * across_x)
    uplift = jnp.dot(
        along, across, precision=lax.Precision.HIGHEST, preferred_element_type=jnp.float32
    )
    mine_owner = lax.dynamic_slice_in_dim(owner_list[:, 0], device * count, count)
    owners = owner_list[:, 0].reshape(n_patch, n_sub, count)
    blocks = block_list.reshape(n_patch, n_sub, count)
    wanted_owner = lax.dynamic_index_in_dim(owners, me_sub, 1, keepdims=False)
    wanted_block = lax.dynamic_index_in_dim(blocks, me_sub, 1, keepdims=False)
    matches = (wanted_owner == me_patch).astype(jnp.int32)
    order = jnp.cumsum(matches, axis=1) - 1
    slots = jnp.arange(capacity, dtype=jnp.int32)
    select = matches[:, None, :] * (order[:, None, :] == slots[None, :, None]).astype(jnp.int32)
    chosen = jnp.sum(select * wanted_block[:, None, :], axis=2)
    filled = jnp.sum(select, axis=2).astype(jnp.float32)
    outgoing = (
        topography[chosen.reshape(-1)].reshape(n_patch, capacity, FP, cols_f)
        * filled[:, :, None, None]
    )
    incoming = lax.all_to_all(outgoing, "patch", split_axis=0, concat_axis=0, tiled=True)
    positions = jnp.arange(count, dtype=jnp.int32)
    earlier = (mine_owner[None, :] == mine_owner[:, None]) & (
        positions[None, :] < positions[:, None]
    )
    rank = jnp.sum(earlier.astype(jnp.int32), axis=1)
    flat = incoming.reshape(n_patch * capacity, FP, cols_f)
    depth_f = flat[mine_owner * capacity + rank].reshape(rows_f, cols_f)
    eta_start = eta_c + uplift
    ones_c = jnp.ones((rows_c, cols_c), jnp.float32)
    first_col = cols_c - cols_f // 2
    fine_uplift = jnp.repeat(jnp.repeat(uplift[:, first_col:], 2, 0), 2, 1)
    wet = wet_f.astype(jnp.float32)
    eta_fine = eta_f + fine_uplift
    statics_c = rims(depth_c, ones_c)
    zero_ghost = jnp.zeros((rows_c,), jnp.float32)
    eta_c1, u_c1, v_c1 = advance(eta_start, u_c, v_c, depth_c, ones_c, statics_c, zero_ghost, 0.0)
    ghost_old = jnp.repeat(eta_start[:, first_col - 1], 2)
    ghost_new = jnp.repeat(eta_c1[:, first_col - 1], 2)
    statics_f = rims(depth_f, wet)
    eta, u, v = (eta_fine, u_f, v_f)
    for step in range(2):
        ghost = ghost_old + (step + 1) / 2.0 * (ghost_new - ghost_old)
        eta, u, v = advance(eta, u, v, depth_f, wet, statics_f, ghost, 1.0)
    return (eta_c1, u_c1, v_c1, eta, u, v)


def solution(mesh):
    placed = (
        P(("runs", "patch", "sub"), None),
        P(("runs", "patch", "sub"), None),
        P(("runs", "patch", "sub"), None),
        P(("runs", "patch", "sub"), None),
        P(("runs", "patch", "sub"), None),
        P(("runs", "patch", "sub"), None),
        P(("runs", "patch", "sub"), None),
        P(("runs", "patch", "sub"), None),
        P(("runs", "patch", "sub"), None, None),
        P("runs", None),
        P("runs"),
        P(("runs", "patch", "sub")),
        P(("runs", "patch", "sub")),
        P(("runs", "patch", "sub")),
        P(("runs", "patch", "sub")),
    )
    return jax.shard_map(
        on_device,
        mesh=mesh,
        in_specs=placed,
        out_specs=(
            P(("runs", "patch", "sub"), None),
            P(("runs", "patch", "sub"), None),
            P(("runs", "patch", "sub"), None),
            P(("runs", "patch", "sub"), None),
            P(("runs", "patch", "sub"), None),
            P(("runs", "patch", "sub"), None),
        ),
        check_vma=False,
    )
```

profile of v0, /device:TPU:17, one launch (start us, length us, event | category | flops | bytes accessed | tf_op | source)
XLA Modules:
  0.0 149.0 jit_solution(2857899705928771187)
XLA Ops:
  1.2 1.4 reduce.11
  4.9 3.5 %gather_fusion = f32[384,2,512]{2,1,0:T(2,128)S(1)} fusion(f32[96,2,512]{2,1,0:T(2,128)S(1)} %copy-done, s32[1024]{0:T(1024)S(1)} %pad_clamp_fusion.1), kind=kCustom, calls=%fused_computation | custom fusion | bytes 3147264 | tf_op jit(solution)/shard_map/gather | solution.py:105
  8.4 1.8 %broadcast_multiply_fusion = f32[8,48,2,512]{3,2,1,0:T(2,128)} fusion(f32[8,48,2,512]{3,2,1,0:T(2,128)S(1)} %bitcast.39, f32[8,48]{1,0:T(8,128)S(1)} %convert_element_type.24), kind=kLoop, calls=%fused_computation.40 | loop fusion | flops 393216 | bytes 3147264 | tf_op jit(solution)/shard_map/mul | solution.py:105
  10.2 5.8 %all-to-all-start = ((f32[8,48,2,512]{3,2,1,0:T(2,128)}), f32[8,48,2,512]{3,2,1,0:T(2,128)}, u32[]{:S(2)}, u32[]{:S(2)}) async-start(f32[8,48,2,512]{3,2,1,0:T(2,128)} %broadcast_multiply_fusion), calls=%async_computation | async-start | bytes 3145728 | tf_op jit(solution)/shard_map/all_to_all | solution.py:108
  16.0 4.2 %collective-permute-start = (f32[2,768]{1,0:T(2,128)S(1)}, f32[2,768]{1,0:T(2,128)S(1)}, u32[]{:S(2)}, u32[]{:S(2)}) collective-permute-start(f32[2,768]{1,0:T(2,128)S(1)} %concatenate.74), channel_id=1, source_target_pairs={{0,1},{1,2},{2,3},{3,4},{4,5},{5,6},{6,7},{7,8},{8,9},{9,10},{10,1... | collective-permute-start | bytes 18440 | tf_op jit(solution)/shard_map/ppermute | solution.py:15
  22.4 46.9 %all-reduce.11 = (f32[256]{0:T(256)S(1)}, f32[256]{0:T(256)S(1)}, f32[256]{0:T(256)S(1)}, f32[256]{0:T(256)S(1)}) all-reduce(f32[256]{0:T(256)S(1)} %dynamic-update-slice.1, f32[256]{0:T(256)S(1)} %dynamic-update-slice.3, f32[256]{0:T(256)S(1)} %dynamic-update-slice.2, ...), channel_id=1, replica_groups=mesh['runs'=2,'patch'=8,'sub'=2] {'patch','sub'}, use_global_device_ids=true, to_apply=%add.8 | all-reduce | flops 1024 | bytes 8192
  69.3 1.8 %fusion.66 = (f32[192,768]{1,0:T(8,128)S(1)}, f32[192,768]{1,0:T(8,128)}) fusion(f32[192,768]{1,0:T(8,128)S(1)} %copy-done.20, f32[256]{0:T(256)S(1)} %get-tuple-element.32, f32[256]{0:T(256)S(1)} %get-tuple-element.33, f32[256]{0:T(256)S(1)} %get-tuple-element.34, f32[256]{0:T(256)S(1)} %get-tuple-element.35, f32[192]{0:T(256)S(1)} %iota_add_fusion), kind=kOutput, calls=%fused_computation.106 | convolution fusion | flops 454557696 | bytes 1774336 | tf_op jit(solution)/shard_map/dot_general | solution.py:90
  71.8 1.9 %collective-permute-start.1 = (f32[1,768]{1,0:T(1,128)}, f32[1,768]{1,0:T(1,128)}, u32[]{:S(2)}, u32[]{:S(2)}) collective-permute-start(f32[1,768]{1,0:T(1,128)} %slice.192), channel_id=1, source_target_pairs={{0,1},{1,2},{2,3},{3,4},{4,5},{5,6},{6,7},{7,8},{8,9},{9,10},{10,1... | collective-permute-start | bytes 9224 | tf_op jit(solution)/shard_map/ppermute | solution.py:15
  75.8 1.4 reshape.148
  77.2 1.2 add.122
  79.3 1.9 %collective-permute-start.4 = (f32[1,512]{0,1:T(8,128)}, f32[1,512]{0,1:T(8,128)}, u32[]{:S(2)}, u32[]{:S(2)}) collective-permute-start(f32[1,512]{0,1:T(8,128)} %slice.214), channel_id=1, source_target_pairs={{0,1},{1,2},{2,3},{3,4},{4,5},{5,6},{6,7},{7,8},{8,9},{9,10},{10,1... | collective-permute-start | bytes 6152 | tf_op jit(solution)/shard_map/ppermute | solution.py:15
  84.0 3.0 %maximum_multiply_fusion = (f32[192,768]{1,0:T(8,128)}, f32[192,768]{1,0:T(8,128)}, f32[192,768]{1,0:T(8,128)S(1)}, f32[192,768]{1,0:T(8,128)}) fusion(f32[192,767]{1,0:T(8,128)S(1)} %add_multiply_fusion, f32[192,1]{1,0:T(8,128)S(1)} %slice.142, f32[768]{0:T(1024)S(1)} %copy-done.18, f32[192,768]{1,0:T(8,128)} %param.16, ...), kind=kLoop, calls=%fused_computation.47 | loop fusion | flops 2211840 | bytes 7083264 | tf_op jit(solution)/shard_map/mul | solution.py:25
  87.6 3.4 %collective-permute-start.2 = (f32[1,768]{1,0:T(1,128)}, f32[1,768]{1,0:T(1,128)S(1)}, u32[]{:S(2)}, u32[]{:S(2)}) collective-permute-start(f32[1,768]{1,0:T(1,128)} %slice.196), channel_id=1, source_target_pairs={{1,0},{2,1},{3,2},{4,3},{5,4},{6,5},{7,6},{8,7},{9,8},{10,9},{11,1... | collective-permute-start | bytes 9224 | tf_op jit(solution)/shard_map/ppermute | solution.py:15
  94.0 2.3 %copy.68 = f32[384,512]{0,1:T(8,128)} copy(f32[384,512]{1,0:T(8,128)} %param.21) | data formatting | bytes 1572864 | tf_op args[6]
  96.5 1.2 slice.195
  97.7 1.3 slice.190
  100.5 2.9 %gather_fusion.1 = f32[192,2,512]{2,1,0:T(2,128)S(1)} fusion(f32[384,2,512]{2,1,0:T(2,128)} %bitcast.4, s32[1024]{0:T(1024)S(1)} %pad_clamp_fusion), kind=kCustom, calls=%fused_computation.1 | custom fusion | bytes 1573632 | tf_op jit(solution)/shard_map/gather | solution.py:115
  103.4 1.4 reshape.155
  104.8 1.4 copy.60
  107.4 2.4 %collective-permute-start.3 = (f32[2,512]{0,1:T(8,128)S(1)}, f32[2,512]{0,1:T(8,128)S(1)}, u32[]{:S(2)}, u32[]{:S(2)}) collective-permute-start(f32[2,512]{0,1:T(8,128)S(1)} %pad_maximum_fusion.3), channel_id=1, source_target_pairs={{0,1},{1,2},{2,3},{3,4},{4,5},{5,6},{6,7},{7,8},{8,9},{9,10},{10,1... | collective-permute-start | bytes 12296 | tf_op jit(solution)/shard_map/ppermute | solution.py:15
  110.0 3.0 %collective-permute-done.3 = f32[2,512]{0,1:T(8,128)S(1)} collective-permute-done((f32[2,512]{0,1:T(8,128)S(1)}, f32[2,512]{0,1:T(8,128)S(1)}, u32[]{:S(2)}, u32[]{:S(2)}) %collective-permute-start.3) | collective-permute-done | bytes 4128 | tf_op jit(solution)/shard_map/ppermute | solution.py:15
  113.1 1.8 %fusion.31 = (f32[384,512]{0,1:T(8,128)S(1)}, f32[384,512]{0,1:T(8,128)S(1)}, f32[384,512]{0,1:T(8,128)S(1)}, f32[384,512]{0,1:T(8,128)S(1)}) fusion(f32[384,511]{0,1:T(8,128)S(1)} %get-tuple-element.65, f32[384,1]{0,1:T(1,128)S(1)} %slice.200, f32[384,511]{0,1:T(8,128)S(1)} %get-tuple-element.64, f32[384,1]{0,1:T(1,128)S(1)} %slice.206, ...), kind=kLoop, calls=%fused_computation.46 | loop fusion | flops 3932160 | bytes 11796480 | tf_op jit(solution)/shard_map/mul | solution.py:25
  115.0 7.6 %collective-permute-start.5 = (f32[1,512]{0,1:T(8,128)S(1)}, f32[1,512]{0,1:T(8,128)S(1)}, u32[]{:S(2)}, u32[]{:S(2)}) collective-permute-start(f32[1,512]{0,1:T(8,128)S(1)} %slice.219), channel_id=1, source_target_pairs={{1,0},{2,1},{3,2},{4,3},{5,4},{6,5},{7,6},{8,7},{9,8},{10,9},{11,1... | collective-permute-start | bytes 6152 | tf_op jit(solution)/shard_map/ppermute | solution.py:15
  124.2 1.9 %collective-permute-start.6 = (f32[1,512]{0,1:T(8,128)S(1)}, f32[1,512]{0,1:T(8,128)S(1)}, u32[]{:S(2)}, u32[]{:S(2)}) collective-permute-start(f32[1,512]{0,1:T(8,128)S(1)} %slice.222), channel_id=1, source_target_pairs={{0,1},{1,2},{2,3},{3,4},{4,5},{5,6},{6,7},{7,8},{8,9},{9,10},{10,1... | collective-permute-start | bytes 6152 | tf_op jit(solution)/shard_map/ppermute | solution.py:15
  126.1 3.7 %collective-permute-done.6 = f32[1,512]{0,1:T(8,128)S(1)} collective-permute-done((f32[1,512]{0,1:T(8,128)S(1)}, f32[1,512]{0,1:T(8,128)S(1)}, u32[]{:S(2)}, u32[]{:S(2)}) %collective-permute-start.6) | collective-permute-done | bytes 2080 | tf_op jit(solution)/shard_map/ppermute | solution.py:15
  129.9 2.3 %fusion.30 = (f32[384,512]{0,1:T(8,128)}, f32[384,512]{0,1:T(8,128)}, f32[384,512]{0,1:T(8,128)S(1)}, f32[384,512]{0,1:T(8,128)}) fusion(f32[384,511]{0,1:T(8,128)S(1)} %get-tuple-element.65, f32[384,1]{0,1:T(1,128)S(1)} %slice.200, f32[384,511]{0,1:T(8,128)S(1)} %get-tuple-element.64, f32[384,1]{0,1:T(1,128)S(1)} %slice.206, ...), kind=kLoop, calls=%fused_computation.45 | loop fusion | flops 3932160 | bytes 11796480 | tf_op jit(solution)/shard_map/mul | solution.py:25
  132.9 7.9 %collective-permute-start.7 = (f32[1,512]{0,1:T(8,128)}, f32[1,512]{0,1:T(8,128)}, u32[]{:S(2)}, u32[]{:S(2)}) collective-permute-start(f32[1,512]{0,1:T(8,128)} %slice.225), channel_id=1, source_target_pairs={{1,0},{2,1},{3,2},{4,3},{5,4},{6,5},{7,6},{8,7},{9,8},{10,9},{11,1... | collective-permute-start | bytes 6152 | tf_op jit(solution)/shard_map/ppermute | solution.py:15
  140.7 1.2 slice.224
  142.0 2.4 %copy.70 = f32[384,512]{1,0:T(8,128)} copy(f32[384,512]{0,1:T(8,128)} %get-tuple-element.37) | data formatting | bytes 1572864
  144.3 1.1 copy.71
  146.6 1.3 fusion.25
  147.9 1.1 copy.69
  (131 shorter events, 20.9 us)
Async XLA Ops:
  0.6 4.3 %copy-start = (f32[96,2,512]{2,1,0:T(2,128)S(1)}, f32[96,2,512]{2,1,0:T(2,128)}, u32[]{:S(2)}) copy-start(f32[96,2,512]{2,1,0:T(2,128)} %param.23) | copy-start | bytes 1179652
  10.2 5.8 %copy-start.3 = (f32[192,768]{1,0:T(8,128)S(1)}, f32[192,768]{1,0:T(8,128)}, u32[]{:S(2)}) copy-start(f32[192,768]{1,0:T(8,128)} %param.18) | copy-start | bytes 1769476
  10.2 10.1 %copy-start.25 = (u32[32]{0:T(128)S(1)}, u32[32]{0:T(128)}, u32[]{:S(2)}) copy-start(u32[32]{0:T(128)} %constant.80) | copy-start | bytes 388
  10.2 11.3 %copy-start.21 = (f32[16]{0:T(128)S(1)}, f32[16]{0:T(128)}, u32[]{:S(2)}) copy-start(f32[16]{0:T(128)} %param.29) | copy-start | bytes 196
  10.2 11.6 %copy-start.22 = (f32[16]{0:T(128)S(1)}, f32[16]{0:T(128)}, u32[]{:S(2)}) copy-start(f32[16]{0:T(128)} %param.27) | copy-start | bytes 196
  10.2 11.8 %copy-start.23 = (f32[16]{0:T(128)S(1)}, f32[16]{0:T(128)}, u32[]{:S(2)}) copy-start(f32[16]{0:T(128)} %param.28) | copy-start | bytes 196
  10.2 12.0 %copy-start.24 = (f32[16]{0:T(128)S(1)}, f32[16]{0:T(128)}, u32[]{:S(2)}) copy-start(f32[16]{0:T(128)} %param.26) | copy-start | bytes 196
  10.2 59.1 %copy-start.20 = (f32[192,768]{1,0:T(8,128)S(1)}, f32[192,768]{1,0:T(8,128)}, u32[]{:S(2)}) copy-start(f32[192,768]{1,0:T(8,128)} %param.15) | copy-start | bytes 1769476
  10.2 90.2 %all-to-all-start = ((f32[8,48,2,512]{3,2,1,0:T(2,128)}), f32[8,48,2,512]{3,2,1,0:T(2,128)}, u32[]{:S(2)}, u32[]{:S(2)}) async-start(f32[8,48,2,512]{3,2,1,0:T(2,128)} %broadcast_multiply_fusion), calls=%async_computation | async-start | bytes 3145728 | tf_op jit(solution)/shard_map/all_to_all | solution.py:108
  16.0 67.9 %collective-permute-start = (f32[2,768]{1,0:T(2,128)S(1)}, f32[2,768]{1,0:T(2,128)S(1)}, u32[]{:S(2)}, u32[]{:S(2)}) collective-permute-start(f32[2,768]{1,0:T(2,128)S(1)} %concatenate.74), channel_id=1, source_target_pairs={{0,1},{1,2},{2,3},{3,4},{4,5},{5,6},{6,7},{7,8},{8,9},{9,10},{10,1... | collective-permute-start | bytes 18440 | tf_op jit(solution)/shard_map/ppermute | solution.py:15
  69.3 4.4 %copy-start.15 = (f32[384,512]{1,0:T(8,128)S(1)}, f32[384,512]{1,0:T(8,128)}, u32[]{:S(2)}) copy-start(f32[384,512]{1,0:T(8,128)} %param.19) | copy-start | bytes 2359300
  71.2 12.8 %copy-start.4 = (f32[192,768]{1,0:T(8,128)}, f32[192,768]{1,0:T(8,128)S(1)}, u32[]{:S(2)}) copy-start(f32[192,768]{1,0:T(8,128)S(1)} %get-tuple-element.62) | copy-start | bytes 1769476
  71.8 12.2 %collective-permute-start.1 = (f32[1,768]{1,0:T(1,128)}, f32[1,768]{1,0:T(1,128)}, u32[]{:S(2)}, u32[]{:S(2)}) collective-permute-start(f32[1,768]{1,0:T(1,128)} %slice.192), channel_id=1, source_target_pairs={{0,1},{1,2},{2,3},{3,4},{4,5},{5,6},{6,7},{7,8},{8,9},{9,10},{10,1... | collective-permute-start | bytes 9224 | tf_op jit(solution)/shard_map/ppermute | solution.py:15
  78.4 5.5 %copy-start.18 = (f32[768]{0:T(1024)S(1)}, f32[768]{0:T(1024)}, u32[]{:S(2)}) copy-start(f32[768]{0:T(1024)} %constant.24.clone.1) | copy-start | bytes 9220
  79.3 33.8 %collective-permute-start.4 = (f32[1,512]{0,1:T(8,128)}, f32[1,512]{0,1:T(8,128)}, u32[]{:S(2)}, u32[]{:S(2)}) collective-permute-start(f32[1,512]{0,1:T(8,128)} %slice.214), channel_id=1, source_target_pairs={{0,1},{1,2},{2,3},{3,4},{4,5},{5,6},{6,7},{7,8},{8,9},{9,10},{10,1... | collective-permute-start | bytes 6152 | tf_op jit(solution)/shard_map/ppermute | solution.py:15
  84.0 7.0 %copy-start.16 = (s32[384,512]{1,0:T(8,128)S(1)}, s32[384,512]{1,0:T(8,128)}, u32[]{:S(2)}) copy-start(s32[384,512]{1,0:T(8,128)} %param.22) | copy-start | bytes 2359300
  87.0 4.0 %copy-start.7 = (f32[192,768]{1,0:T(8,128)}, f32[192,768]{1,0:T(8,128)S(1)}, u32[]{:S(2)}) copy-start(f32[192,768]{1,0:T(8,128)S(1)} %get-tuple-element.54) | copy-start | bytes 1769476
  87.6 11.4 %collective-permute-start.2 = (f32[1,768]{1,0:T(1,128)}, f32[1,768]{1,0:T(1,128)S(1)}, u32[]{:S(2)}, u32[]{:S(2)}) collective-permute-start(f32[1,768]{1,0:T(1,128)} %slice.196), channel_id=1, source_target_pairs={{1,0},{2,1},{3,2},{4,3},{5,4},{6,5},{7,6},{8,7},{9,8},{10,9},{11,1... | collective-permute-start | bytes 9224 | tf_op jit(solution)/shard_map/ppermute | solution.py:15
  91.3 21.8 %copy-start.1 = (s32[384,512]{0,1:T(8,128)}, s32[384,512]{0,1:T(8,128)S(1)}, u32[]{:S(2)}) copy-start(s32[384,512]{0,1:T(8,128)S(1)} %copy.64) | copy-start | bytes 2359300
  92.8 3.4 %copy-start.19 = (f32[192]{0:T(256)S(1)}, f32[192]{0:T(256)}, u32[]{:S(2)}) copy-start(f32[192]{0:T(256)} %slice_reduce_fusion.1) | copy-start | bytes 2308
  96.2 2.8 %copy-start.5 = (f32[192,768]{1,0:T(8,128)S(1)}, f32[192,768]{1,0:T(8,128)}, u32[]{:S(2)}) copy-start(f32[192,768]{1,0:T(8,128)} %copy-done.4) | copy-start | bytes 1769476
  96.5 2.5 %copy-start.8 = (f32[192,768]{1,0:T(8,128)S(1)}, f32[192,768]{1,0:T(8,128)}, u32[]{:S(2)}) copy-start(f32[192,768]{1,0:T(8,128)} %copy-done.7) | copy-start | bytes 1769476
  96.5 2.5 %copy-start.9 = (f32[192,768]{1,0:T(8,128)S(1)}, f32[192,768]{1,0:T(8,128)}, u32[]{:S(2)}) copy-start(f32[192,768]{1,0:T(8,128)} %get-tuple-element.46) | copy-start | bytes 1769476
  107.4 5.6 %collective-permute-start.3 = (f32[2,512]{0,1:T(8,128)S(1)}, f32[2,512]{0,1:T(8,128)S(1)}, u32[]{:S(2)}, u32[]{:S(2)}) collective-permute-start(f32[2,512]{0,1:T(8,128)S(1)} %pad_maximum_fusion.3), channel_id=1, source_target_pairs={{0,1},{1,2},{2,3},{3,4},{4,5},{5,6},{6,7},{7,8},{8,9},{9,10},{10,1... | collective-permute-start | bytes 12296 | tf_op jit(solution)/shard_map/ppermute | solution.py:15
  109.8 3.3 %copy-start.11 = (f32[384,512]{0,1:T(8,128)S(1)}, f32[384,512]{0,1:T(8,128)}, u32[]{:S(2)}) copy-start(f32[384,512]{0,1:T(8,128)} %copy.68) | copy-start | bytes 2359300
  110.0 3.1 %copy-start.10 = (f32[384,512]{0,1:T(8,128)S(1)}, f32[384,512]{0,1:T(8,128)}, u32[]{:S(2)}) copy-start(f32[384,512]{0,1:T(8,128)} %copy.63) | copy-start | bytes 2359300
  115.0 8.7 %collective-permute-start.5 = (f32[1,512]{0,1:T(8,128)S(1)}, f32[1,512]{0,1:T(8,128)S(1)}, u32[]{:S(2)}, u32[]{:S(2)}) collective-permute-start(f32[1,512]{0,1:T(8,128)S(1)} %slice.219), channel_id=1, source_target_pairs={{1,0},{2,1},{3,2},{4,3},{5,4},{6,5},{7,6},{8,7},{9,8},{10,9},{11,1... | collective-permute-start | bytes 6152 | tf_op jit(solution)/shard_map/ppermute | solution.py:15
  122.9 7.0 %copy-start.2 = (s32[384,512]{0,1:T(8,128)S(1)}, s32[384,512]{0,1:T(8,128)}, u32[]{:S(2)}) copy-start(s32[384,512]{0,1:T(8,128)} %copy-done.1) | copy-start | bytes 2359300
  124.2 5.7 %collective-permute-start.6 = (f32[1,512]{0,1:T(8,128)S(1)}, f32[1,512]{0,1:T(8,128)S(1)}, u32[]{:S(2)}, u32[]{:S(2)}) collective-permute-start(f32[1,512]{0,1:T(8,128)S(1)} %slice.222), channel_id=1, source_target_pairs={{0,1},{1,2},{2,3},{3,4},{4,5},{5,6},{6,7},{7,8},{8,9},{9,10},{10,1... | collective-permute-start | bytes 6152 | tf_op jit(solution)/shard_map/ppermute | solution.py:15
  132.9 11.4 %copy-start.12 = (f32[384,512]{0,1:T(8,128)S(1)}, f32[384,512]{0,1:T(8,128)}, u32[]{:S(2)}) copy-start(f32[384,512]{0,1:T(8,128)} %get-tuple-element.51) | copy-start | bytes 2359300
  132.9 12.6 %collective-permute-start.7 = (f32[1,512]{0,1:T(8,128)}, f32[1,512]{0,1:T(8,128)}, u32[]{:S(2)}, u32[]{:S(2)}) collective-permute-start(f32[1,512]{0,1:T(8,128)} %slice.225), channel_id=1, source_target_pairs={{1,0},{2,1},{3,2},{4,3},{5,4},{6,5},{7,6},{8,7},{9,8},{10,9},{11,1... | collective-permute-start | bytes 6152 | tf_op jit(solution)/shard_map/ppermute | solution.py:15
  141.9 3.5 %copy-start.6 = (f32[384,512]{0,1:T(8,128)S(1)}, f32[384,512]{0,1:T(8,128)}, u32[]{:S(2)}) copy-start(f32[384,512]{0,1:T(8,128)} %get-tuple-element.36) | copy-start | bytes 2359300
  (3 other events, 3.5 us)
where the time goes:
time: 150 us; the launch traced here: 149 us
  blocking collectives  46.9 us (31%)
  local copies, waits for them, and re-layouts  37.1 us (25%)
  starting transfers between devices  36.9 us (25%)
  other arithmetic  16.9 us (11%)
  waiting for transfers between devices  7.51 us (5%)
  between operations  1.98 us (1%)
  matrix products  1.84 us (1%)
    unnamed x1, blocking collectives  46.9 us
    ppermute x8, starting transfers between devices, shifted(): return lax.ppermute(block, axis, route)  31.1 us
    unnamed x70, local copies, waits for them, and re-layouts  13.2 us
    ppermute x8, waiting for transfers between devices, shifted(): return lax.ppermute(block, axis, route)  7.51 us
    mul x3, other arithmetic, west_faces(): flux_x = h_west * u_new  7.09 us
    all_to_all x1, starting transfers between devices, on_device(): lax.all_to_all(outgoing, 'patch', split_axis=0, concat_axis=0, tiled=True)  5.75 us
    gather x1, local copies, waits for them, and re-layouts, on_device(): topography[chosen.reshape(-1)].reshape(n_patch, capacity, FP, cols_f)  3.46 us
  transfers between devices with their start and end apart: 9, of which 3 were waited for; matrix products, arithmetic and copies ran while one was open for 24% of the time, Pallas kernels for 0%

commit v1 on v0

v1 whole, which is shorter than its diff:
```python
import functools

import jax
import jax.numpy as jnp
from jax import lax
from jax.experimental import pallas as pl
from jax.experimental.pallas import tpu as pltpu
from jax.sharding import PartitionSpec as P

FP = 2
LANES = 128
PAD = 16
HALO = 8
CH = 16
KB = 256
PARTS = 2

courant = 0.35


def west(x):
    return pltpu.roll(x, 1, 1)


def east(x):
    return pltpu.roll(x, x.shape[1] - 1, 1)


def south_of(ref, b, here):
    edge = ref[pl.ds(pl.multiple_of(b - 8, 8), 8)]
    return pltpu.roll(jnp.concatenate([edge, here], 0), 1, 0)[8:]


def north_of(ref, b, here):
    edge = ref[pl.ds(pl.multiple_of(b + CH, 8), 8)]
    return pltpu.roll(jnp.concatenate([here, edge], 0), CH + 7, 0)[:CH]


def ring_position(p, n):
    odd = p % 2
    return (1 - odd) * (p // 2) + odd * (n - 1 - p // 2)


def ring_patch(k, n):
    back = k // (n // 2)
    return (1 - back) * (2 * k) + back * (2 * (n - 1 - k) + 1)


def kernel(
    n_patch,
    n_sub,
    src_ref,
    faults_ref,
    eta_c_in,
    u_c_in,
    v_c_in,
    depth_c_in,
    eta_f_in,
    u_f_in,
    v_f_in,
    wet_f_in,
    topo_in,
    eta_c_out,
    u_c_out,
    v_c_out,
    eta_f_out,
    u_f_out,
    v_f_out,
    gath,
    fbuf,
    fpar,
    etac,
    uc,
    vc,
    hc,
    gc,
    etac1,
    etaf,
    uf,
    vf,
    wetf,
    wet,
    mwf,
    mmf,
    hf,
    hwf,
    hsf,
    gf,
    etap,
    ghost1,
    ghost2,
    local_sem,
    out_sem,
    ring_send,
    ring_recv,
    fault_send,
    fault_recv,
    halo_send,
    halo_recv,
    rim_send,
    rim_recv,
):
    mesh_id = pl.DeviceIdType.MESH
    patch = lax.axis_index("patch")
    sub = lax.axis_index("sub")
    n = n_patch * n_sub
    me = patch * n_sub + sub
    rows_c, cols_c = eta_c_in.shape
    rows_f, cols_f = eta_f_in.shape
    held = topo_in.shape[0]
    first_col = cols_c - cols_f // 2

    def where(flat):
        return {"patch": flat // n_sub, "sub": flat % n_sub}

    own_topo = pltpu.make_async_copy(
        topo_in, gath.at[pl.ds(patch * held, held)], local_sem.at[8]
    )
    own_topo.start()
    pairs = [
        (eta_c_in, etac),
        (u_c_in, uc),
        (v_c_in, vc),
        (depth_c_in, hc),
        (eta_f_in, etaf),
        (u_f_in, uf),
        (v_f_in, vf),
        (wet_f_in, wet),
    ]
    loads = []
    for i, (src, dst) in enumerate(pairs):
        copy = pltpu.make_async_copy(
            src, dst.at[pl.ds(PAD, src.shape[0])], local_sem.at[i]
        )
        copy.start()
        loads.append(copy)

    barrier = pltpu.get_barrier_semaphore()

    def greet(i, carry):
        pl.semaphore_signal(
            barrier, inc=1, device_id=where((me + i) % n), device_id_type=mesh_id
        )
        return carry

    lax.fori_loop(1, n, greet, 0)
    for ref in (etac, hc, gc, etac1, etaf, hf, gf, wet, etap):
        rows = ref.shape[0]
        zero = jnp.zeros((PAD - HALO, ref.shape[1]), ref.dtype)
        ref[0 : PAD - HALO] = zero
        ref[rows - (PAD - HALO) : rows] = zero
    pl.semaphore_wait(barrier, n - 1)

    here = ring_position(patch, n_patch)
    following = ring_patch((here + 1) % n_patch, n_patch)
    before = ring_patch((here + n_patch - 1) % n_patch, n_patch)
    piece = held // (2 * PARTS)

    def ring_copy(way, part, step):
        if way == 0:
            owner = ring_patch((here + n_patch - step) % n_patch, n_patch)
            target = following
        else:
            owner = ring_patch((here + step) % n_patch, n_patch)
            target = before
        block = gath.at[pl.ds(owner * held + (way * PARTS + part) * piece, piece)]
        index = (way * PARTS + part) * (n_patch - 1) + step
        return pltpu.make_async_remote_copy(
            src_ref=block,
            dst_ref=block,
            send_sem=ring_send.at[index],
            recv_sem=ring_recv.at[index],
            device_id={"patch": target, "sub": sub},
            device_id_type=mesh_id,
        )

    def ring_step(step, part):
        for way in (0, 1):
            ring_copy(way, part, step - 1).wait_recv()
            ring_copy(way, part, step).start()

    own_topo.wait()
    for part in range(PARTS):
        for way in (0, 1):
            ring_copy(way, part, 0).start()

    def fault_copy(i):
        return pltpu.make_async_remote_copy(
            src_ref=faults_ref,
            dst_ref=fbuf.at[me],
            send_sem=fault_send.at[i - 1],
            recv_sem=fault_recv.at[i - 1],
            device_id=where((me + i) % n),
            device_id_type=mesh_id,
        )

    def send_fault(i, carry):
        fault_copy(i).start()
        return carry

    lax.fori_loop(1, n, send_fault, 0)

    halos = []
    north, south = where((me + 1) % n), where((me + n - 1) % n)
    for i, (src, dst) in enumerate(pairs):
        rows = src.shape[0]
        up = pltpu.make_async_remote_copy(
            src_ref=src.at[pl.ds(rows - HALO, HALO)],
            dst_ref=dst.at[pl.ds(PAD - HALO, HALO)],
            send_sem=halo_send.at[2 * i],
            recv_sem=halo_recv.at[2 * i],
            device_id=north,
            device_id_type=mesh_id,
        )
        down = pltpu.make_async_remote_copy(
            src_ref=src.at[pl.ds(0, HALO)],
            dst_ref=dst.at[pl.ds(PAD + rows, HALO)],
            send_sem=halo_send.at[2 * i + 1],
            recv_sem=halo_recv.at[2 * i + 1],
            device_id=south,
            device_id_type=mesh_id,
        )
        up.start()
        down.start()
        halos.append((up, down))

    def arrived(indices):
        for i in indices:
            loads[i].wait()
            for copy in halos[i]:
                copy.wait_recv()

    def gather_faults():
        fbuf[me] = faults_ref[...]

        def wait_fault(i, carry):
            fault_copy(i).wait_recv()
            return carry

        lax.fori_loop(1, n, wait_fault, 0)
        per_tile = n * LANES // fpar.shape[1]
        for t in range(fpar.shape[1] // LANES):
            fpar[:, t * LANES : (t + 1) * LANES] = jnp.sum(
                fbuf[t * per_tile : (t + 1) * per_tile], axis=0
            )

    def add_uplift(eta, rows_at, cols_at):
        total = eta.shape[0]
        width = eta.shape[1]

        def block(kb, carry):
            at = pl.ds(pl.multiple_of(kb * KB, KB), KB)
            centre_row = fpar[0:1, at]
            centre_col = fpar[1:2, at]
            widths = fpar[2:3, at]
            slips = fpar[3:4, at]
            y = rows_at(lax.broadcasted_iota(jnp.int32, (total, KB), 0))
            along_y = (y.astype(jnp.float32) - centre_row) / widths
            along = jnp.exp(-along_y * along_y) * slips
            x = cols_at(lax.broadcasted_iota(jnp.int32, (width, KB), 0))
            across_x = (x.astype(jnp.float32) - centre_col) / widths
            across = (1.0 + across_x) * jnp.exp(-across_x * across_x)
            eta[...] += lax.dot_general(
                along,
                across,
                (((1,), (1,)), ((), ())),
                precision=lax.Precision.HIGHEST,
                preferred_element_type=jnp.float32,
            )
            return carry

        if fpar.shape[1] == KB:
            block(0, 0)
        else:
            lax.fori_loop(0, fpar.shape[1] // KB, block, 0)

    def coarse_uplift():
        arrived([0])
        add_uplift(etac, lambda i: me * rows_c + i - PAD, lambda i: i)

    def fine_uplift():
        arrived([4])
        add_uplift(
            etaf, lambda i: me * rows_c + i // 2 - PAD // 2, lambda i: first_col + i // 2
        )

    def chunks(body, first, last):
        def step(i, carry):
            body(pl.multiple_of(first + i * CH, 8))
            return carry

        lax.fori_loop(0, (last - first) // CH, step, 0)

    lo_c, hi_c = PAD - HALO, PAD + rows_c + HALO
    lo_f, hi_f = PAD - HALO, PAD + rows_f + HALO

    def coarse_faces():
        arrived([1, 2, 3])

        def body(b):
            at = pl.ds(pl.multiple_of(b, 8), CH)
            col = lax.broadcasted_iota(jnp.int32, (CH, cols_c), 1)
            row = lax.broadcasted_iota(jnp.int32, (CH, cols_c), 0) + (
                me * rows_c + b - PAD
            )
            eta, h = etac[at], hc[at]
            u = jnp.where(col > 0, uc[at] - courant * (eta - west(eta)), 0.0)
            flux_x = 0.5 * (h + west(h)) * u
            v = vc[at] - courant * (eta - south_of(etac, b, eta))
            v = jnp.where((row >= 1) & (row < n * rows_c), v, 0.0)
            flux_y = 0.5 * (h + south_of(hc, b, h)) * v
            uc[at] = u
            vc[at] = v
            gc[at] = flux_y
            etac1[at] = eta - courant * (east(flux_x) - flux_x - flux_y)

        chunks(body, lo_c, hi_c)

    outs = []

    def write(src, dst):
        copy = pltpu.make_async_copy(
            src.at[pl.ds(PAD, dst.shape[0])], dst, out_sem.at[len(outs)]
        )
        copy.start()
        outs.append(copy)

    def coarse_eta():
        def body(b):
            at = pl.ds(pl.multiple_of(b, 8), CH)
            etac1[at] = etac1[at] - courant * north_of(gc, b, gc[at])

        chunks(body, lo_c, hi_c)
        write(etac1, eta_c_out)
        write(uc, u_c_out)
        write(vc, v_c_out)

    def ghosts():
        rows = ghost1.shape[0]
        coarse = lax.broadcasted_iota(jnp.int32, (rows, etac.shape[0]), 1)
        fine = lax.broadcasted_iota(jnp.int32, (rows, etac.shape[0]), 0)
        spread = (coarse == fine // 2 + PAD // 2).astype(jnp.float32)
        old = etac[:, first_col - LANES : first_col]
        new = etac1[:, first_col - LANES : first_col]
        for ref, value in ((ghost1, old + 0.5 * (new - old)), (ghost2, new)):
            ref[...] = west(
                jnp.dot(
                    spread,
                    value,
                    precision=lax.Precision.HIGHEST,
                    preferred_element_type=jnp.float32,
                )
            )

    def eta_west(eta, ghost, col):
        return jnp.where(
            col == 0, jnp.concatenate([ghost] * (cols_f // LANES), 1), west(eta)
        )

    def fine_masks():
        arrived([5, 6, 7])
        wet[lo_f:PAD] = wet[lo_f:PAD] * (me + n - 1) // n
        wet[PAD + rows_f : hi_f] = wet[PAD + rows_f : hi_f] * (
            (2 * n - 2 - me) // n
        )
        wetf[...] = wet[...].astype(jnp.float32)

    def fine_first():
        def body(b):
            at = pl.ds(pl.multiple_of(b, 8), CH)
            col = lax.broadcasted_iota(jnp.int32, (CH, cols_f), 1)
            m = wetf[at]
            mw = m * jnp.where(col == 0, 1.0, west(m))
            mm = m * south_of(wetf, b, m)
            eta = etaf[at]
            mwf[at] = mw
            mmf[at] = mm
            uf[at] = (uf[at] - courant * (eta - eta_west(eta, ghost1[at], col))) * mw
            vf[at] = (vf[at] - courant * (eta - south_of(etaf, b, eta))) * mm

        chunks(body, lo_f, hi_f)

    work = [
        gather_faults,
        coarse_uplift,
        coarse_faces,
        coarse_eta,
        ghosts,
        fine_uplift,
        fine_masks,
        fine_first,
    ]
    shown = min(n_patch - 1, 7)
    for step in range(1, shown):
        for part in range(PARTS):
            if work:
                work.pop(0)()
            ring_step(step, part)
    for piece_of_work in work:
        piece_of_work()
    if shown < n_patch - 1:

        def later(step, carry):
            for part in range(PARTS):
                ring_step(step, part)
            return carry

        lax.fori_loop(shown, n_patch - 1, later, 0)
    for part in range(PARTS):
        for way in (0, 1):
            ring_copy(way, part, n_patch - 2).wait_recv()

    def take(i, carry):
        blocks = [gath[src_ref[i * 4 + j]] for j in range(4)]
        row = pl.multiple_of(PAD + i * 8, 8)
        for t in range(cols_f // LANES):
            hf[pl.ds(row, 8), t * LANES : (t + 1) * LANES] = jnp.concatenate(
                [b[t * FP : (t + 1) * FP] for b in blocks], 0
            )
        return carry

    lax.fori_loop(0, rows_f // 8, take, 0)
    rims = []
    for i, (first, to, target) in enumerate(
        ((PAD + rows_f - HALO, PAD - HALO, north), (PAD, PAD + rows_f, south))
    ):
        copy = pltpu.make_async_remote_copy(
            src_ref=hf.at[pl.ds(first, HALO)],
            dst_ref=hf.at[pl.ds(to, HALO)],
            send_sem=rim_send.at[i],
            recv_sem=rim_recv.at[i],
            device_id=target,
            device_id_type=mesh_id,
        )
        copy.start()
        rims.append(copy)
    for copy in rims:
        copy.wait()

    def fine_flux(b):
        at = pl.ds(pl.multiple_of(b, 8), CH)
        col = lax.broadcasted_iota(jnp.int32, (CH, cols_f), 1)
        h = hf[at]
        hw = jnp.where(col == 0, h, 0.5 * (h + west(h)))
        hs = 0.5 * (h + south_of(hf, b, h))
        flux_x = hw * uf[at]
        flux_y = hs * vf[at]
        hwf[at] = hw
        hsf[at] = hs
        gf[at] = flux_y
        flux_east = jnp.where(col == cols_f - 1, 0.0, east(flux_x))
        etaf[at] = etaf[at] - courant * (flux_east - flux_x - flux_y)

    chunks(fine_flux, lo_f, hi_f)

    def fine_eta(b):
        at = pl.ds(pl.multiple_of(b, 8), CH)
        etaf[at] = etaf[at] - courant * north_of(gf, b, gf[at])

    chunks(fine_eta, lo_f, hi_f)

    def fine_second(b):
        at = pl.ds(pl.multiple_of(b, 8), CH)
        col = lax.broadcasted_iota(jnp.int32, (CH, cols_f), 1)
        eta = etaf[at]
        u = (uf[at] - courant * (eta - eta_west(eta, ghost2[at], col))) * mwf[at]
        v = (vf[at] - courant * (eta - south_of(etaf, b, eta))) * mmf[at]
        flux_x = hwf[at] * u
        flux_y = hsf[at] * v
        uf[at] = u
        vf[at] = v
        gf[at] = flux_y
        flux_east = jnp.where(col == cols_f - 1, 0.0, east(flux_x))
        etap[at] = eta - courant * (flux_east - flux_x - flux_y)

    chunks(fine_second, lo_f, hi_f)
    write(uf, u_f_out)
    write(vf, v_f_out)

    def fine_last(b):
        at = pl.ds(pl.multiple_of(b, 8), CH)
        etap[at] = etap[at] - courant * north_of(gf, b, gf[at])

    chunks(fine_last, PAD, PAD + rows_f)
    write(etap, eta_f_out)

    def sent(i, carry):
        fault_copy(i).wait_send()
        return carry

    lax.fori_loop(1, n, sent, 0)
    for up, down in halos:
        up.wait_send()
        down.wait_send()

    def passed(step, carry):
        for part in range(PARTS):
            for way in (0, 1):
                ring_copy(way, part, step).wait_send()
        return carry

    lax.fori_loop(0, n_patch - 1, passed, 0)
    for copy in outs:
        copy.wait()


def on_device(
    eta_c,
    u_c,
    v_c,
    depth_c,
    eta_f,
    u_f,
    v_f,
    wet_f,
    topography,
    owner_list,
    block_list,
    fault_row,
    fault_col,
    fault_width,
    fault_slip,
):
    rows_c, cols_c = eta_c.shape
    rows_f, cols_f = eta_f.shape
    n_patch = lax.axis_size("patch")
    n_sub = lax.axis_size("sub")
    n = n_patch * n_sub
    count = rows_f // FP
    held = topography.shape[0]
    mine = fault_row.shape[0]
    device = lax.axis_index(("patch", "sub"))
    source = lax.dynamic_slice_in_dim(
        owner_list[:, 0], device * count, count
    ) * held + lax.dynamic_slice_in_dim(block_list, device * count, count)
    per_tile = LANES // mine
    params = jnp.stack([fault_row, fault_col, fault_width, fault_slip])
    lane = jnp.arange(LANES) // mine
    faults = jnp.where(
        lane[None, :] == device % per_tile, jnp.tile(params, (2, per_tile)), 0.0
    )
    tiles = (
        topography.reshape(held, FP, cols_f // LANES, LANES)
        .transpose(0, 2, 1, 3)
        .reshape(held, FP * cols_f // LANES, LANES)
    )
    f32 = jnp.float32
    coarse = pltpu.VMEM((rows_c + 2 * PAD, cols_c), f32)
    fine = pltpu.VMEM((rows_f + 2 * PAD, cols_f), f32)
    dma = pltpu.SemaphoreType.DMA
    any_spec = pl.BlockSpec(memory_space=pl.ANY)
    return pl.pallas_call(
        functools.partial(kernel, n_patch, n_sub),
        out_shape=[jax.ShapeDtypeStruct((rows_c, cols_c), f32)] * 3
        + [jax.ShapeDtypeStruct((rows_f, cols_f), f32)] * 3,
        in_specs=[
            pl.BlockSpec(memory_space=pltpu.SMEM),
            pl.BlockSpec(memory_space=pltpu.VMEM),
        ]
        + [any_spec] * 9,
        out_specs=[any_spec] * 6,
        scratch_shapes=[
            pltpu.VMEM((n_patch * held,) + tiles.shape[1:], f32),
            pltpu.VMEM((n, 8, LANES), f32),
            pltpu.VMEM((8, n * mine), f32),
        ]
        + [coarse] * 6
        + [fine] * 4
        + [pltpu.VMEM((rows_f + 2 * PAD, cols_f), jnp.int32)]
        + [fine] * 7
        + [pltpu.VMEM((rows_f + 2 * PAD, LANES), f32)] * 2
        + [
            dma((9,)),
            dma((6,)),
            dma((2 * PARTS * (n_patch - 1),)),
            dma((2 * PARTS * (n_patch - 1),)),
            dma((n - 1,)),
            dma((n - 1,)),
            dma((16,)),
            dma((16,)),
            dma((2,)),
            dma((2,)),
        ],
        compiler_params=pltpu.CompilerParams(
            collective_id=0, has_side_effects=True, vmem_limit_bytes=60 * 2**20
        ),
    )(
        source,
        faults,
        eta_c,
        u_c,
        v_c,
        depth_c,
        eta_f,
        u_f,
        v_f,
        wet_f,
        tiles,
    )


def solution(mesh):
    rows = P(("runs", "patch", "sub"), None)
    line = P(("runs", "patch", "sub"))
    return jax.shard_map(
        on_device,
        mesh=mesh,
        in_specs=(rows,) * 8
        + (P(("runs", "patch", "sub"), None, None), P("runs", None), P("runs"))
        + (line,) * 4,
        out_specs=(rows,) * 6,
        check_vma=False,
    )
```

time: 150 us -> 70.1 us (0.47)
  the two profiles are of different devices: /device:TPU:17 before, /device:TPU:0 now
where the time goes in v1:
time: 70.1 us; the launch traced here: 69 us
  Pallas kernels  57.1 us (81%)
  local copies, waits for them, and re-layouts  8.41 us (12%)
  other arithmetic  2.76 us (4%)
  between operations  0.72 us (1%)
    pallas_call x1, Pallas kernels, on_device(): pl.pallas_call(functools.partial(kernel, n_patch, n_sub), out_shape=[jax....  57.1 us
    unnamed x24, local copies, waits for them, and re-layouts  8.33 us

profile of v1, /device:TPU:0, one launch (start us, length us, event | category | flops | bytes accessed | tf_op | source)
XLA Modules:
  0.0 69.0 jit_solution(14218744018206415427)
XLA Ops:
  0.7 0.8 %dynamic-slice_multiply_fusion = s32[192,1]{0,1:T(1,128)S(1)} fusion(s32[3072,1]{0,1:T(1,128)} %param.24, s32[]{:T(128)S(6)} %select_n.24), kind=kLoop, calls=%fused_computation.7 | loop fusion | flops 192 | bytes 1540 | tf_op jit(solution)/shard_map/mul | solution.py:533
  1.4 0.0 copy-start.5
  1.4 0.0 copy-start.6
  1.4 0.0 copy-start.7
  1.4 0.0 copy-start.8
  1.4 1.4 %dynamic-slice_add_fusion.src_ref = s32[192]{0:T(256)} fusion(s32[192]{0:T(256)S(1)} %bitcast.13, s32[3072]{0:T(1024)} %param.25, s32[]{:T(128)S(6)} %select_n.24), kind=kLoop, calls=%fused_computation.6 | loop fusion | flops 192 | bytes 2308 | tf_op jit(solution)/shard_map/add | solution.py:533
  2.8 0.0 copy-done.5
  2.8 0.0 copy-done.6
  2.8 0.0 copy-done.7
  2.8 0.0 copy-done.8
  2.9 0.1 tile.10
  2.9 0.6 broadcast_select_fusion.faults_ref
  3.5 57.1 %shard_map.190 = (f32[192,768]{1,0:T(8,128)}, f32[192,768]{1,0:T(8,128)}, f32[192,768]{1,0:T(8,128)}, f32[384,512]{1,0:T(8,128)}, f32[384,512]{1,0:T(8,128)}, /*index=5*/f32[384,512]{1,0:T(8,128)}) custom-call(s32[192]{0:T(256)} %dynamic-slice_add_fusion.src_ref, f32[8,128]{1,0:T(8,128)} %broadcast_select_fusion.faults_ref, f32[192,768]{1,0:T(8,128)} %eta_c_in.1, ...), custom_call_target="tpu_custom_call" | custom-call | tf_op jit(solution)/shard_map/pallas_call | solution.py:552
  60.7 0.0 copy-start.4
  60.7 2.0 %copy.28 = f32[192,768]{1,0:T(8,128)} copy(f32[192,768]{1,0:T(8,128)} %get-tuple-element.12) | data formatting | bytes 1179648
  62.7 0.0 copy-done.4
  62.7 0.0 copy-start.3
  62.7 0.8 %copy.29 = f32[192,768]{1,0:T(8,128)} copy(f32[192,768]{1,0:T(8,128)S(1)} %copy-done.4) | data formatting | bytes 1179648
  63.5 0.5 copy-done.3
  64.0 0.0 copy-start.2
  64.0 0.8 %copy.30 = f32[192,768]{1,0:T(8,128)} copy(f32[192,768]{1,0:T(8,128)S(1)} %copy-done.3) | data formatting | bytes 1179648
  64.8 0.5 copy-done.2
  65.3 0.0 copy-start.1
  65.3 0.9 %copy.31 = f32[384,512]{1,0:T(8,128)} copy(f32[384,512]{1,0:T(8,128)S(1)} %copy-done.2) | data formatting | bytes 1572864
  66.2 0.5 copy-done.1
  66.7 0.0 copy-start
  66.7 0.9 %copy.32 = f32[384,512]{1,0:T(8,128)} copy(f32[384,512]{1,0:T(8,128)S(1)} %copy-done.1) | data formatting | bytes 1572864
  67.6 0.5 copy-done
  68.2 0.9 %copy.33 = f32[384,512]{1,0:T(8,128)} copy(f32[384,512]{1,0:T(8,128)S(1)} %copy-done) | data formatting | bytes 1572864
  (3 shorter events, 0.0 us)
Async XLA Ops:
  1.4 1.4 %copy-start.5 = (f32[16]{0:T(128)S(1)}, f32[16]{0:T(128)}, u32[]{:S(2)}) copy-start(f32[16]{0:T(128)} %param.29) | copy-start | bytes 196
  1.4 1.4 %copy-start.6 = (f32[16]{0:T(128)S(1)}, f32[16]{0:T(128)}, u32[]{:S(2)}) copy-start(f32[16]{0:T(128)} %param.28) | copy-start | bytes 196
  1.4 1.4 %copy-start.7 = (f32[16]{0:T(128)S(1)}, f32[16]{0:T(128)}, u32[]{:S(2)}) copy-start(f32[16]{0:T(128)} %param.27) | copy-start | bytes 196
  1.4 1.4 %copy-start.8 = (f32[16]{0:T(128)S(1)}, f32[16]{0:T(128)}, u32[]{:S(2)}) copy-start(f32[16]{0:T(128)} %param.26) | copy-start | bytes 196
  60.7 2.0 %copy-start.4 = (f32[192,768]{1,0:T(8,128)S(1)}, f32[192,768]{1,0:T(8,128)}, u32[]{:S(2)}) copy-start(f32[192,768]{1,0:T(8,128)} %get-tuple-element.13) | copy-start | bytes 1769476
  62.7 1.3 %copy-start.3 = (f32[192,768]{1,0:T(8,128)S(1)}, f32[192,768]{1,0:T(8,128)}, u32[]{:S(2)}) copy-start(f32[192,768]{1,0:T(8,128)} %get-tuple-element.14) | copy-start | bytes 1769476
  64.0 1.3 %copy-start.2 = (f32[384,512]{1,0:T(8,128)S(1)}, f32[384,512]{1,0:T(8,128)}, u32[]{:S(2)}) copy-start(f32[384,512]{1,0:T(8,128)} %get-tuple-element.15) | copy-start | bytes 2359300
  65.3 1.4 %copy-start.1 = (f32[384,512]{1,0:T(8,128)S(1)}, f32[384,512]{1,0:T(8,128)}, u32[]{:S(2)}) copy-start(f32[384,512]{1,0:T(8,128)} %get-tuple-element.16) | copy-start | bytes 2359300
  66.7 1.4 %copy-start = (f32[384,512]{1,0:T(8,128)S(1)}, f32[384,512]{1,0:T(8,128)}, u32[]{:S(2)}) copy-start(f32[384,512]{1,0:T(8,128)} %get-tuple-element.17) | copy-start | bytes 2359300

commit v2 on v1

--- a/solution.py
+++ b/solution.py
@@ -14,6 +14,7 @@
 CH = 16
 KB = 256
 PARTS = 2
+SLABS = 2
 
 courant = 0.35
 
@@ -31,9 +32,9 @@
     return pltpu.roll(jnp.concatenate([edge, here], 0), 1, 0)[8:]
 
 
-def north_of(ref, b, here):
-    edge = ref[pl.ds(pl.multiple_of(b + CH, 8), 8)]
-    return pltpu.roll(jnp.concatenate([here, edge], 0), CH + 7, 0)[:CH]
+def north_of(here, above):
+    rows = here.shape[0]
+    return pltpu.roll(jnp.concatenate([here, above], 0), rows + 7, 0)[:rows]
 
 
 def ring_position(p, n):
@@ -49,8 +50,9 @@
 def kernel(
     n_patch,
     n_sub,
-    src_ref,
-    faults_ref,
+    owner_in,
+    block_in,
+    faults_in,
     eta_c_in,
     u_c_in,
     v_c_in,
@@ -66,6 +68,9 @@
     eta_f_out,
     u_f_out,
     v_f_out,
+    owners,
+    blocks,
+    faults_ref,
     gath,
     fbuf,
     fpar,
@@ -73,7 +78,6 @@
     uc,
     vc,
     hc,
-    gc,
     etac1,
     etaf,
     uf,
@@ -85,8 +89,8 @@
     hf,
     hwf,
     hsf,
-    gf,
     etap,
+    rim,
     ghost1,
     ghost2,
     local_sem,
@@ -135,6 +139,12 @@
         copy.start()
         loads.append(copy)
 
+    lists = []
+    for i, (src, dst) in enumerate(((owner_in, owners), (block_in, blocks))):
+        copy = pltpu.make_async_copy(src, dst, local_sem.at[9 + i])
+        copy.start()
+        lists.append(copy)
+
     barrier = pltpu.get_barrier_semaphore()
 
     def greet(i, carry):
@@ -144,7 +154,11 @@
         return carry
 
     lax.fori_loop(1, n, greet, 0)
-    for ref in (etac, hc, gc, etac1, etaf, hf, gf, wet, etap):
+    per_tile = LANES * n // fpar.shape[1]
+    faults_ref[...] = pltpu.roll(
+        faults_in[...], (me % per_tile) * (LANES // per_tile), 1
+    )
+    for ref in (etac, hc, etac1, etaf, hf, wet):
         rows = ref.shape[0]
         zero = jnp.zeros((PAD - HALO, ref.shape[1]), ref.dtype)
         ref[0 : PAD - HALO] = zero
@@ -238,7 +252,6 @@
             return carry
 
         lax.fori_loop(1, n, wait_fault, 0)
-        per_tile = n * LANES // fpar.shape[1]
         for t in range(fpar.shape[1] // LANES):
             fpar[:, t * LANES : (t + 1) * LANES] = jnp.sum(
                 fbuf[t * per_tile : (t + 1) * per_tile], axis=0
@@ -284,21 +297,22 @@
             etaf, lambda i: me * rows_c + i // 2 - PAD // 2, lambda i: first_col + i // 2
         )
 
-    def chunks(body, first, last):
+    def chunks(body, first, last, cols):
+        count = (last - first) // CH
+
         def step(i, carry):
-            body(pl.multiple_of(first + i * CH, 8))
-            return carry
-
-        lax.fori_loop(0, (last - first) // CH, step, 0)
+            return body(pl.multiple_of(first + (count - 1 - i) * CH, 8), carry)
+
+        lax.fori_loop(0, count, step, jnp.zeros((8, cols), jnp.float32))
 
     lo_c, hi_c = PAD - HALO, PAD + rows_c + HALO
     lo_f, hi_f = PAD - HALO, PAD + rows_f + HALO
 
-    def coarse_faces():
+    def coarse_step():
         arrived([1, 2, 3])
 
-        def body(b):
-            at = pl.ds(pl.multiple_of(b, 8), CH)
+        def body(b, flux_above):
+            at = pl.ds(b, CH)
             col = lax.broadcasted_iota(jnp.int32, (CH, cols_c), 1)
             row = lax.broadcasted_iota(jnp.int32, (CH, cols_c), 0) + (
                 me * rows_c + b - PAD
@@ -311,10 +325,14 @@
             flux_y = 0.5 * (h + south_of(hc, b, h)) * v
             uc[at] = u
             vc[at] = v
-            gc[at] = flux_y
-            etac1[at] = eta - courant * (east(flux_x) - flux_x - flux_y)
-
-        chunks(body, lo_c, hi_c)
+            spread = east(flux_x) - flux_x + north_of(flux_y, flux_above) - flux_y
+            etac1[at] = eta - courant * spread
+            return flux_y[:8]
+
+        chunks(body, lo_c, hi_c, cols_c)
+        write(etac1, eta_c_out)
+        write(uc, u_c_out)
+        write(vc, v_c_out)
 
     outs = []
 
@@ -324,16 +342,6 @@
         )
         copy.start()
         outs.append(copy)
-
-    def coarse_eta():
-        def body(b):
-            at = pl.ds(pl.multiple_of(b, 8), CH)
-            etac1[at] = etac1[at] - courant * north_of(gc, b, gc[at])
-
-        chunks(body, lo_c, hi_c)
-        write(etac1, eta_c_out)
-        write(uc, u_c_out)
-        write(vc, v_c_out)
 
     def ghosts():
         rows = ghost1.shape[0]
@@ -366,8 +374,8 @@
         wetf[...] = wet[...].astype(jnp.float32)
 
     def fine_first():
-        def body(b):
-            at = pl.ds(pl.multiple_of(b, 8), CH)
+        def body(b, carry):
+            at = pl.ds(b, CH)
             col = lax.broadcasted_iota(jnp.int32, (CH, cols_f), 1)
             m = wetf[at]
             mw = m * jnp.where(col == 0, 1.0, west(m))
@@ -377,14 +385,14 @@
             mmf[at] = mm
             uf[at] = (uf[at] - courant * (eta - eta_west(eta, ghost1[at], col))) * mw
             vf[at] = (vf[at] - courant * (eta - south_of(etaf, b, eta))) * mm
-
-        chunks(body, lo_f, hi_f)
+            return carry
+
+        chunks(body, lo_f, hi_f, cols_f)
 
     work = [
         gather_faults,
         coarse_uplift,
-        coarse_faces,
-        coarse_eta,
+        coarse_step,
         ghosts,
         fine_uplift,
         fine_masks,
@@ -410,35 +418,45 @@
         for way in (0, 1):
             ring_copy(way, part, n_patch - 2).wait_recv()
 
-    def take(i, carry):
-        blocks = [gath[src_ref[i * 4 + j]] for j in range(4)]
-        row = pl.multiple_of(PAD + i * 8, 8)
+    for copy in lists:
+        copy.wait()
+    count = rows_f // FP
+
+    def take(first, dst, row):
+        tiles = [
+            gath[owners[first + j] * held + blocks[first + j]] for j in range(4)
+        ]
         for t in range(cols_f // LANES):
-            hf[pl.ds(row, 8), t * LANES : (t + 1) * LANES] = jnp.concatenate(
-                [b[t * FP : (t + 1) * FP] for b in blocks], 0
+            dst[pl.ds(row, 8), t * LANES : (t + 1) * LANES] = jnp.concatenate(
+                [b[t * FP : (t + 1) * FP] for b in tiles], 0
             )
-        return carry
-
-    lax.fori_loop(0, rows_f // 8, take, 0)
+
+    mate = patch * n_sub + (n_sub - 1 - sub)
+    take((mate * count + n * count - 4) % (n * count), rim, 0)
+    take((mate * count + count) % (n * count), rim, 8)
     rims = []
-    for i, (first, to, target) in enumerate(
-        ((PAD + rows_f - HALO, PAD - HALO, north), (PAD, PAD + rows_f, south))
-    ):
+    for i, to in enumerate((PAD - HALO, PAD + rows_f)):
         copy = pltpu.make_async_remote_copy(
-            src_ref=hf.at[pl.ds(first, HALO)],
+            src_ref=rim.at[pl.ds(i * HALO, HALO)],
             dst_ref=hf.at[pl.ds(to, HALO)],
             send_sem=rim_send.at[i],
             recv_sem=rim_recv.at[i],
-            device_id=target,
+            device_id={"patch": patch, "sub": n_sub - 1 - sub},
             device_id_type=mesh_id,
         )
         copy.start()
         rims.append(copy)
+
+    def take_own(i, carry):
+        take(me * count + i * 4, hf, pl.multiple_of(PAD + i * 8, 8))
+        return carry
+
+    lax.fori_loop(0, rows_f // 8, take_own, 0, unroll=4)
     for copy in rims:
         copy.wait()
 
-    def fine_flux(b):
-        at = pl.ds(pl.multiple_of(b, 8), CH)
+    def fine_flux(b, flux_above):
+        at = pl.ds(b, CH)
         col = lax.broadcasted_iota(jnp.int32, (CH, cols_f), 1)
         h = hf[at]
         hw = jnp.where(col == 0, h, 0.5 * (h + west(h)))
@@ -447,20 +465,15 @@
         flux_y = hs * vf[at]
         hwf[at] = hw
         hsf[at] = hs
-        gf[at] = flux_y
         flux_east = jnp.where(col == cols_f - 1, 0.0, east(flux_x))
-        etaf[at] = etaf[at] - courant * (flux_east - flux_x - flux_y)
-
-    chunks(fine_flux, lo_f, hi_f)
-
-    def fine_eta(b):
-        at = pl.ds(pl.multiple_of(b, 8), CH)
-        etaf[at] = etaf[at] - courant * north_of(gf, b, gf[at])
-
-    chunks(fine_eta, lo_f, hi_f)
-
-    def fine_second(b):
-        at = pl.ds(pl.multiple_of(b, 8), CH)
+        spread = flux_east - flux_x + north_of(flux_y, flux_above) - flux_y
+        etaf[at] = etaf[at] - courant * spread
+        return flux_y[:8]
+
+    chunks(fine_flux, lo_f, hi_f, cols_f)
+
+    def fine_second(b, flux_above):
+        at = pl.ds(b, CH)
         col = lax.broadcasted_iota(jnp.int32, (CH, cols_f), 1)
         eta = etaf[at]
         u = (uf[at] - courant * (eta - eta_west(eta, ghost2[at], col))) * mwf[at]
@@ -469,19 +482,14 @@
         flux_y = hsf[at] * v
         uf[at] = u
         vf[at] = v
-        gf[at] = flux_y
         flux_east = jnp.where(col == cols_f - 1, 0.0, east(flux_x))
-        etap[at] = eta - courant * (flux_east - flux_x - flux_y)
-
-    chunks(fine_second, lo_f, hi_f)
+        spread = flux_east - flux_x + north_of(flux_y, flux_above) - flux_y
+        etap[at] = eta - courant * spread
+        return flux_y[:8]
+
+    chunks(fine_second, lo_f, hi_f, cols_f)
     write(uf, u_f_out)
     write(vf, v_f_out)
-
-    def fine_last(b):
-        at = pl.ds(pl.multiple_of(b, 8), CH)
-        etap[at] = etap[at] - courant * north_of(gf, b, gf[at])
-
-    chunks(fine_last, PAD, PAD + rows_f)
     write(etap, eta_f_out)
 
     def sent(i, carry):
@@ -501,6 +509,34 @@
 
     lax.fori_loop(0, n_patch - 1, passed, 0)
     for copy in outs:
+        copy.wait()
+
+
+def hand_over(*refs):
+    results, outputs, staged = refs[:6], refs[6:12], refs[12:18]
+    read_sem, write_sem = refs[18:]
+    reads, writes = [], []
+    for i in (2, 1, 0, 5, 4, 3):
+        rows = results[i].shape[0] // SLABS
+        for j in range(SLABS):
+            at = pl.ds(j * rows, rows)
+            k = i * SLABS + j
+            reads.append(
+                pltpu.make_async_copy(
+                    results[i].at[at], staged[i].at[at], read_sem.at[k]
+                )
+            )
+            writes.append(
+                pltpu.make_async_copy(
+                    staged[i].at[at], outputs[i].at[at], write_sem.at[k]
+                )
+            )
+    for copy in reads:
+        copy.start()
+    for read, write in zip(reads, writes):
+        read.wait()
+        write.start()
+    for copy in writes:
         copy.wait()
 
 
@@ -526,19 +562,10 @@
     n_patch = lax.axis_size("patch")
     n_sub = lax.axis_size("sub")
     n = n_patch * n_sub
-    count = rows_f // FP
     held = topography.shape[0]
     mine = fault_row.shape[0]
-    device = lax.axis_index(("patch", "sub"))
-    source = lax.dynamic_slice_in_dim(
-        owner_list[:, 0], device * count, count
-    ) * held + lax.dynamic_slice_in_dim(block_list, device * count, count)
-    per_tile = LANES // mine
     params = jnp.stack([fault_row, fault_col, fault_width, fault_slip])
-    lane = jnp.arange(LANES) // mine
-    faults = jnp.where(
-        lane[None, :] == device % per_tile, jnp.tile(params, (2, per_tile)), 0.0
-    )
+    faults = jnp.pad(params, ((0, 4), (0, LANES - mine)))
     tiles = (
         topography.reshape(held, FP, cols_f // LANES, LANES)
         .transpose(0, 2, 1, 3)
@@ -549,28 +576,30 @@
     fine = pltpu.VMEM((rows_f + 2 * PAD, cols_f), f32)
     dma = pltpu.SemaphoreType.DMA
     any_spec = pl.BlockSpec(memory_space=pl.ANY)
-    return pl.pallas_call(
+    results = pl.pallas_call(
         functools.partial(kernel, n_patch, n_sub),
         out_shape=[jax.ShapeDtypeStruct((rows_c, cols_c), f32)] * 3
         + [jax.ShapeDtypeStruct((rows_f, cols_f), f32)] * 3,
-        in_specs=[
-            pl.BlockSpec(memory_space=pltpu.SMEM),
-            pl.BlockSpec(memory_space=pltpu.VMEM),
-        ]
+        in_specs=[any_spec] * 2
+        + [pl.BlockSpec(memory_space=pltpu.VMEM)]
         + [any_spec] * 9,
         out_specs=[any_spec] * 6,
         scratch_shapes=[
+            pltpu.SMEM(block_list.shape, jnp.int32),
+            pltpu.SMEM(block_list.shape, jnp.int32),
+            pltpu.VMEM((8, LANES), f32),
             pltpu.VMEM((n_patch * held,) + tiles.shape[1:], f32),
             pltpu.VMEM((n, 8, LANES), f32),
             pltpu.VMEM((8, n * mine), f32),
         ]
-        + [coarse] * 6
+        + [coarse] * 5
         + [fine] * 4
         + [pltpu.VMEM((rows_f + 2 * PAD, cols_f), jnp.int32)]
-        + [fine] * 7
+        + [fine] * 6
+        + [pltpu.VMEM((2 * HALO, cols_f), f32)]
         + [pltpu.VMEM((rows_f + 2 * PAD, LANES), f32)] * 2
         + [
-            dma((9,)),
+            dma((11,)),
             dma((6,)),
             dma((2 * PARTS * (n_patch - 1),)),
             dma((2 * PARTS * (n_patch - 1),)),
@@ -585,7 +614,8 @@
             collective_id=0, has_side_effects=True, vmem_limit_bytes=60 * 2**20
         ),
     )(
-        source,
+        owner_list.reshape(-1),
+        block_list,
         faults,
         eta_c,
         u_c,
@@ -597,6 +627,15 @@
         wet_f,
         tiles,
     )
+    return pl.pallas_call(
+        hand_over,
+        out_shape=[jax.ShapeDtypeStruct(r.shape, r.dtype) for r in results],
+        in_specs=[any_spec] * 6,
+        out_specs=[any_spec] * 6,
+        scratch_shapes=[pltpu.VMEM(r.shape, r.dtype) for r in results]
+        + [dma((6 * SLABS,))] * 2,
+        compiler_params=pltpu.CompilerParams(vmem_limit_bytes=60 * 2**20),
+    )(*results)
 
 
 def solution(mesh):

time: 70.1 us -> 61.3 us (0.87); the launches traced: 69 us -> 61.1 us
  local copies, waits for them, and re-layouts: 8.41 us -> 0.67 us
  other arithmetic: 2.76 us -> 0.6 us
  Pallas kernels: 57.1 us -> 59.2 us
    unnamed x24 -> x8, local copies, waits for them, and re-layouts: 8.33 us -> 0.67 us
    pallas_call x0 -> x1, Pallas kernels: none -> 3.75 us  [on_device(): pl.pallas_call(hand_over, out_shape=[jax.ShapeDtypeStruct(r.shape, r.dtyp...]
    pallas_call x1, Pallas kernels: 57.1 us -> 55.4 us  [on_device(): pl.pallas_call(functools.partial(kernel, n_patch, n_sub), out_shape=[jax....]
    add x1 -> x0, other arithmetic: 1.37 us -> none  [on_device(): lax.dynamic_slice_in_dim(owner_list[:, 0], device * count, count) * held]
    mul x1 -> x0, other arithmetic: 0.76 us -> none  [on_device(): lax.dynamic_slice_in_dim(owner_list[:, 0], device * count, count) * held]
where the time goes in v2:
time: 61.3 us; the launch traced here: 61.1 us
  Pallas kernels  59.2 us (97%)
  between operations  0.68 us (1%)
  local copies, waits for them, and re-layouts  0.67 us (1%)
    pallas_call x1, Pallas kernels, on_device(): pl.pallas_call(functools.partial(kernel, n_patch, n_sub), out_shape=[jax....  55.4 us
    pallas_call x1, Pallas kernels, on_device(): pl.pallas_call(hand_over, out_shape=[jax.ShapeDtypeStruct(r.shape, r.dtyp...  3.75 us

profile of v2, /device:TPU:0, one launch (start us, length us, event | category | flops | bytes accessed | tf_op | source)
XLA Modules:
  0.0 61.1 jit_solution(6131328797221235269)
XLA Ops:
  0.6 0.0 copy-start.3
  0.6 0.0 copy-start
  0.7 0.0 copy-start.1
  0.7 0.0 copy-start.2
  0.7 0.6 %copy-done.3 = f32[16]{0:T(128)S(1)} copy-done((f32[16]{0:T(128)S(1)}, f32[16]{0:T(128)}, u32[]{:S(2)}) %copy-start.3) | copy-done | bytes 88
  1.3 0.0 copy-done
  1.3 0.0 copy-done.1
  1.3 0.0 copy-done.2
  1.3 0.6 select_maximum_fusion.faults_in
  1.9 55.4 %shard_map.190 = (f32[192,768]{1,0:T(8,128)}, f32[192,768]{1,0:T(8,128)}, f32[192,768]{1,0:T(8,128)}, f32[384,512]{1,0:T(8,128)}, f32[384,512]{1,0:T(8,128)}, /*index=5*/f32[384,512]{1,0:T(8,128)}) custom-call(s32[3072]{0:T(1024)} %bitcast.11, s32[3072]{0:T(1024)} %block_in.1, f32[8,128]{1,0:T(8,128)} %select_maximum_fusion.faults_in, f32[192,768]{1,0:T(8,128)} %eta_c_in.1, ...), custom_call_target="tpu_custom_call" | custom-call | tf_op jit(solution)/shard_map/pallas_call | solution.py:579
  57.4 3.7 %shard_map.191 = (f32[192,768]{1,0:T(8,128)}, f32[192,768]{1,0:T(8,128)}, f32[192,768]{1,0:T(8,128)}, f32[384,512]{1,0:T(8,128)}, f32[384,512]{1,0:T(8,128)}, /*index=5*/f32[384,512]{1,0:T(8,128)}) custom-call(f32[192,768]{1,0:T(8,128)} %get-tuple-element.12.refs_0_, f32[192,768]{1,0:T(8,128)} %get-tuple-element.13.refs_1_, ...), custom_call_target="tpu_custom_call" | custom-call | tf_op jit(solution)/shard_map/pallas_call | solution.py:630
Async XLA Ops:
  0.6 0.7 %copy-start.3 = (f32[16]{0:T(128)S(1)}, f32[16]{0:T(128)}, u32[]{:S(2)}) copy-start(f32[16]{0:T(128)} %param.26) | copy-start | bytes 196
  0.6 0.7 %copy-start = (f32[16]{0:T(128)S(1)}, f32[16]{0:T(128)}, u32[]{:S(2)}) copy-start(f32[16]{0:T(128)} %param.29) | copy-start | bytes 196
  0.7 0.7 %copy-start.1 = (f32[16]{0:T(128)S(1)}, f32[16]{0:T(128)}, u32[]{:S(2)}) copy-start(f32[16]{0:T(128)} %param.28) | copy-start | bytes 196
  0.7 0.7 %copy-start.2 = (f32[16]{0:T(128)S(1)}, f32[16]{0:T(128)}, u32[]{:S(2)}) copy-start(f32[16]{0:T(128)} %param.27) | copy-start | bytes 196

commit v3 on v2

--- a/solution.py
+++ b/solution.py
@@ -11,7 +11,9 @@
 LANES = 128
 PAD = 16
 HALO = 8
-CH = 16
+COARSE_CH = 16
+FINE_CH = 80
+SEGMENTS = 5
 KB = 256
 PARTS = 2
 SLABS = 2
@@ -52,7 +54,10 @@
     n_sub,
     owner_in,
     block_in,
-    faults_in,
+    row_in,
+    col_in,
+    width_in,
+    slip_in,
     eta_c_in,
     u_c_in,
     v_c_in,
@@ -70,6 +75,7 @@
     v_f_out,
     owners,
     blocks,
+    params,
     faults_ref,
     gath,
     fbuf,
@@ -140,7 +146,16 @@
         loads.append(copy)
 
     lists = []
-    for i, (src, dst) in enumerate(((owner_in, owners), (block_in, blocks))):
+    for i, (src, dst) in enumerate(
+        (
+            (owner_in, owners),
+            (block_in, blocks),
+            (row_in, params.at[0]),
+            (col_in, params.at[1]),
+            (width_in, params.at[2]),
+            (slip_in, params.at[3]),
+        )
+    ):
         copy = pltpu.make_async_copy(src, dst, local_sem.at[9 + i])
         copy.start()
         lists.append(copy)
@@ -155,9 +170,16 @@
 
     lax.fori_loop(1, n, greet, 0)
     per_tile = LANES * n // fpar.shape[1]
-    faults_ref[...] = pltpu.roll(
-        faults_in[...], (me % per_tile) * (LANES // per_tile), 1
-    )
+    for copy in lists[2:]:
+        copy.wait()
+    line = lax.broadcasted_iota(jnp.int32, (8, LANES), 0)
+    lane = lax.broadcasted_iota(jnp.int32, (8, LANES), 1)
+    lane = lane - (me % per_tile) * (LANES // per_tile)
+    tile = jnp.zeros((8, LANES), jnp.float32)
+    for i in range(4):
+        for j in range(LANES // per_tile):
+            tile = jnp.where((line == i) & (lane == j), params[i, j], tile)
+    faults_ref[...] = tile
     for ref in (etac, hc, etac1, etaf, hf, wet):
         rows = ref.shape[0]
         zero = jnp.zeros((PAD - HALO, ref.shape[1]), ref.dtype)
@@ -297,13 +319,16 @@
             etaf, lambda i: me * rows_c + i // 2 - PAD // 2, lambda i: first_col + i // 2
         )
 
-    def chunks(body, first, last, cols):
-        count = (last - first) // CH
+    def chunks(body, size, first, last, carry):
+        count = (last - first) // size
 
         def step(i, carry):
-            return body(pl.multiple_of(first + (count - 1 - i) * CH, 8), carry)
-
-        lax.fori_loop(0, count, step, jnp.zeros((8, cols), jnp.float32))
+            return body(pl.multiple_of(first + (count - 1 - i) * size, 8), carry)
+
+        return lax.fori_loop(0, count, step, carry)
+
+    def no_flux(cols):
+        return jnp.zeros((8, cols), jnp.float32)
 
     lo_c, hi_c = PAD - HALO, PAD + rows_c + HALO
     lo_f, hi_f = PAD - HALO, PAD + rows_f + HALO
@@ -312,9 +337,9 @@
         arrived([1, 2, 3])
 
         def body(b, flux_above):
-            at = pl.ds(b, CH)
-            col = lax.broadcasted_iota(jnp.int32, (CH, cols_c), 1)
-            row = lax.broadcasted_iota(jnp.int32, (CH, cols_c), 0) + (
+            at = pl.ds(b, COARSE_CH)
+            col = lax.broadcasted_iota(jnp.int32, (COARSE_CH, cols_c), 1)
+            row = lax.broadcasted_iota(jnp.int32, (COARSE_CH, cols_c), 0) + (
                 me * rows_c + b - PAD
             )
             eta, h = etac[at], hc[at]
@@ -329,16 +354,19 @@
             etac1[at] = eta - courant * spread
             return flux_y[:8]
 
-        chunks(body, lo_c, hi_c, cols_c)
+        chunks(body, COARSE_CH, lo_c, hi_c, no_flux(cols_c))
         write(etac1, eta_c_out)
         write(uc, u_c_out)
         write(vc, v_c_out)
 
     outs = []
 
-    def write(src, dst):
+    def write(src, dst, first=0, last=None):
+        rows = (dst.shape[0] if last is None else last) - first
         copy = pltpu.make_async_copy(
-            src.at[pl.ds(PAD, dst.shape[0])], dst, out_sem.at[len(outs)]
+            src.at[pl.ds(PAD + first, rows)],
+            dst.at[pl.ds(first, rows)],
+            out_sem.at[len(outs)],
         )
         copy.start()
         outs.append(copy)
@@ -375,8 +403,8 @@
 
     def fine_first():
         def body(b, carry):
-            at = pl.ds(b, CH)
-            col = lax.broadcasted_iota(jnp.int32, (CH, cols_f), 1)
+            at = pl.ds(b, FINE_CH)
+            col = lax.broadcasted_iota(jnp.int32, (FINE_CH, cols_f), 1)
             m = wetf[at]
             mw = m * jnp.where(col == 0, 1.0, west(m))
             mm = m * south_of(wetf, b, m)
@@ -387,7 +415,7 @@
             vf[at] = (vf[at] - courant * (eta - south_of(etaf, b, eta))) * mm
             return carry
 
-        chunks(body, lo_f, hi_f, cols_f)
+        chunks(body, FINE_CH, lo_f, hi_f, 0)
 
     work = [
         gather_faults,
@@ -418,7 +446,7 @@
         for way in (0, 1):
             ring_copy(way, part, n_patch - 2).wait_recv()
 
-    for copy in lists:
+    for copy in lists[:2]:
         copy.wait()
     count = rows_f // FP
 
@@ -456,8 +484,8 @@
         copy.wait()
 
     def fine_flux(b, flux_above):
-        at = pl.ds(b, CH)
-        col = lax.broadcasted_iota(jnp.int32, (CH, cols_f), 1)
+        at = pl.ds(b, FINE_CH)
+        col = lax.broadcasted_iota(jnp.int32, (FINE_CH, cols_f), 1)
         h = hf[at]
         hw = jnp.where(col == 0, h, 0.5 * (h + west(h)))
         hs = 0.5 * (h + south_of(hf, b, h))
@@ -470,11 +498,11 @@
         etaf[at] = etaf[at] - courant * spread
         return flux_y[:8]
 
-    chunks(fine_flux, lo_f, hi_f, cols_f)
+    chunks(fine_flux, FINE_CH, lo_f, hi_f, no_flux(cols_f))
 
     def fine_second(b, flux_above):
-        at = pl.ds(b, CH)
-        col = lax.broadcasted_iota(jnp.int32, (CH, cols_f), 1)
+        at = pl.ds(b, FINE_CH)
+        col = lax.broadcasted_iota(jnp.int32, (FINE_CH, cols_f), 1)
         eta = etaf[at]
         u = (uf[at] - courant * (eta - eta_west(eta, ghost2[at], col))) * mwf[at]
         v = (vf[at] - courant * (eta - south_of(etaf, b, eta))) * mmf[at]
@@ -487,10 +515,14 @@
         etap[at] = eta - courant * spread
         return flux_y[:8]
 
-    chunks(fine_second, lo_f, hi_f, cols_f)
-    write(uf, u_f_out)
-    write(vf, v_f_out)
-    write(etap, eta_f_out)
+    carry = no_flux(cols_f)
+    segment = (hi_f - lo_f) // SEGMENTS
+    for k in range(SEGMENTS - 1, -1, -1):
+        first = lo_f + k * segment
+        carry = chunks(fine_second, FINE_CH, first, first + segment, carry)
+        own = (max(first - PAD, 0), min(first + segment - PAD, rows_f))
+        for src, dst in ((uf, u_f_out), (vf, v_f_out), (etap, eta_f_out)):
+            write(src, dst, *own)
 
     def sent(i, carry):
         fault_copy(i).wait_send()
@@ -564,8 +596,6 @@
     n = n_patch * n_sub
     held = topography.shape[0]
     mine = fault_row.shape[0]
-    params = jnp.stack([fault_row, fault_col, fault_width, fault_slip])
-    faults = jnp.pad(params, ((0, 4), (0, LANES - mine)))
     tiles = (
         topography.reshape(held, FP, cols_f // LANES, LANES)
         .transpose(0, 2, 1, 3)
@@ -580,13 +610,12 @@
         functools.partial(kernel, n_patch, n_sub),
         out_shape=[jax.ShapeDtypeStruct((rows_c, cols_c), f32)] * 3
         + [jax.ShapeDtypeStruct((rows_f, cols_f), f32)] * 3,
-        in_specs=[any_spec] * 2
-        + [pl.BlockSpec(memory_space=pltpu.VMEM)]
-        + [any_spec] * 9,
+        in_specs=[any_spec] * 15,
         out_specs=[any_spec] * 6,
         scratch_shapes=[
             pltpu.SMEM(block_list.shape, jnp.int32),
             pltpu.SMEM(block_list.shape, jnp.int32),
+            pltpu.SMEM((4, mine), f32),
             pltpu.VMEM((8, LANES), f32),
             pltpu.VMEM((n_patch * held,) + tiles.shape[1:], f32),
             pltpu.VMEM((n, 8, LANES), f32),
@@ -599,8 +628,8 @@
         + [pltpu.VMEM((2 * HALO, cols_f), f32)]
         + [pltpu.VMEM((rows_f + 2 * PAD, LANES), f32)] * 2
         + [
-            dma((11,)),
-            dma((6,)),
+            dma((15,)),
+            dma((3 + 3 * SEGMENTS,)),
             dma((2 * PARTS * (n_patch - 1),)),
             dma((2 * PARTS * (n_patch - 1),)),
             dma((n - 1,)),
@@ -616,7 +645,10 @@
     )(
         owner_list.reshape(-1),
         block_list,
-        faults,
+        fault_row,
+        fault_col,
+        fault_width,
+        fault_slip,
         eta_c,
         u_c,
         v_c,

time: 61.3 us -> 52.8 us (0.86)
  Pallas kernels: 59.2 us -> 52 us
  local copies, waits for them, and re-layouts: 0.67 us -> 0 us
    pallas_call x1, Pallas kernels: 55.4 us -> 48.3 us  [on_device(): pl.pallas_call(functools.partial(kernel, n_patch, n_sub), out_shape=[jax....]
    unnamed x8 -> x0, local copies, waits for them, and re-layouts: 0.67 us -> none
where the time goes in v3:
time: 52.8 us; the launch traced here: 52.7 us
  Pallas kernels  52 us (98%)
  between operations  0.65 us (1%)
    pallas_call x1, Pallas kernels, on_device(): pl.pallas_call(functools.partial(kernel, n_patch, n_sub), out_shape=[jax....  48.3 us
    pallas_call x1, Pallas kernels, on_device(): pl.pallas_call(hand_over, out_shape=[jax.ShapeDtypeStruct(r.shape, r.dtyp...  3.75 us

profile of v3, /device:TPU:0, one launch (start us, length us, event | category | flops | bytes accessed | tf_op | source)
XLA Modules:
  0.0 52.7 jit_solution(3341319210579218826)
XLA Ops:
  0.6 48.3 %shard_map.190 = (f32[192,768]{1,0:T(8,128)}, f32[192,768]{1,0:T(8,128)}, f32[192,768]{1,0:T(8,128)}, f32[384,512]{1,0:T(8,128)}, f32[384,512]{1,0:T(8,128)}, /*index=5*/f32[384,512]{1,0:T(8,128)}) custom-call(s32[3072]{0:T(1024)} %bitcast.7, s32[3072]{0:T(1024)} %block_in.1, f32[16]{0:T(128)} %row_in.1, f32[16]{0:T(128)} %col_in.1, f32[16]{0:T(128)} %width_in.1, ...), custom_call_target="tpu_custom_call" | custom-call | tf_op jit(solution)/shard_map/pallas_call | solution.py:609
  48.9 3.7 %shard_map.191 = (f32[192,768]{1,0:T(8,128)}, f32[192,768]{1,0:T(8,128)}, f32[192,768]{1,0:T(8,128)}, f32[384,512]{1,0:T(8,128)}, f32[384,512]{1,0:T(8,128)}, /*index=5*/f32[384,512]{1,0:T(8,128)}) custom-call(f32[192,768]{1,0:T(8,128)} %get-tuple-element.12.refs_0_, f32[192,768]{1,0:T(8,128)} %get-tuple-element.13.refs_1_, ...), custom_call_target="tpu_custom_call" | custom-call | tf_op jit(solution)/shard_map/pallas_call | solution.py:662

commit v4 on v3

--- a/solution.py
+++ b/solution.py
@@ -15,7 +15,7 @@
 FINE_CH = 80
 SEGMENTS = 5
 KB = 256
-PARTS = 2
+PARTS = 3
 SLABS = 2
 
 courant = 0.35
@@ -200,9 +200,12 @@
             owner = ring_patch((here + step) % n_patch, n_patch)
             target = before
         block = gath.at[pl.ds(owner * held + (way * PARTS + part) * piece, piece)]
+        source = block
+        if isinstance(step, int) and step == 0:
+            source = topo_in.at[pl.ds((way * PARTS + part) * piece, piece)]
         index = (way * PARTS + part) * (n_patch - 1) + step
         return pltpu.make_async_remote_copy(
-            src_ref=block,
+            src_ref=source,
             dst_ref=block,
             send_sem=ring_send.at[index],
             recv_sem=ring_recv.at[index],
@@ -215,7 +218,6 @@
             ring_copy(way, part, step - 1).wait_recv()
             ring_copy(way, part, step).start()
 
-    own_topo.wait()
     for part in range(PARTS):
         for way in (0, 1):
             ring_copy(way, part, 0).start()
@@ -429,7 +431,7 @@
     shown = min(n_patch - 1, 7)
     for step in range(1, shown):
         for part in range(PARTS):
-            if work:
+            if work and part < 2:
                 work.pop(0)()
             ring_step(step, part)
     for piece_of_work in work:
@@ -445,6 +447,8 @@
     for part in range(PARTS):
         for way in (0, 1):
             ring_copy(way, part, n_patch - 2).wait_recv()
+
+    own_topo.wait()
 
     for copy in lists[:2]:
         copy.wait()
@@ -484,8 +488,8 @@
         copy.wait()
 
     def fine_flux(b, flux_above):
-        at = pl.ds(b, FINE_CH)
-        col = lax.broadcasted_iota(jnp.int32, (FINE_CH, cols_f), 1)
+        at = pl.ds(b, 2 * FINE_CH + 40)
+        col = lax.broadcasted_iota(jnp.int32, (2 * FINE_CH + 40, cols_f), 1)
         h = hf[at]
         hw = jnp.where(col == 0, h, 0.5 * (h + west(h)))
         hs = 0.5 * (h + south_of(hf, b, h))
@@ -498,7 +502,7 @@
         etaf[at] = etaf[at] - courant * spread
         return flux_y[:8]
 
-    chunks(fine_flux, FINE_CH, lo_f, hi_f, no_flux(cols_f))
+    chunks(fine_flux, 2 * FINE_CH + 40, lo_f, hi_f, no_flux(cols_f))
 
     def fine_second(b, flux_above):
         at = pl.ds(b, FINE_CH)

time: 52.8 us -> 51.8 us (0.981)
  Pallas kernels: 52 us -> 51 us
    pallas_call x1, Pallas kernels: 48.3 us -> 47.3 us  [on_device(): pl.pallas_call(functools.partial(kernel, n_patch, n_sub), out_shape=[jax....]
where the time goes in v4:
time: 51.8 us; the launch traced here: 51.7 us
  Pallas kernels  51 us (98%)
  between operations  0.65 us (1%)
    pallas_call x1, Pallas kernels, on_device(): pl.pallas_call(functools.partial(kernel, n_patch, n_sub), out_shape=[jax....  47.3 us
    pallas_call x1, Pallas kernels, on_device(): pl.pallas_call(hand_over, out_shape=[jax.ShapeDtypeStruct(r.shape, r.dtyp...  3.75 us

profile of v4, /device:TPU:0, one launch (start us, length us, event | category | flops | bytes accessed | tf_op | source)
XLA Modules:
  0.0 51.7 jit_solution(1811261580409546488)
XLA Ops:
  0.6 47.3 %shard_map.190 = (f32[192,768]{1,0:T(8,128)}, f32[192,768]{1,0:T(8,128)}, f32[192,768]{1,0:T(8,128)}, f32[384,512]{1,0:T(8,128)}, f32[384,512]{1,0:T(8,128)}, /*index=5*/f32[384,512]{1,0:T(8,128)}) custom-call(s32[3072]{0:T(1024)} %bitcast.7, s32[3072]{0:T(1024)} %block_in.1, f32[16]{0:T(128)} %row_in.1, f32[16]{0:T(128)} %col_in.1, f32[16]{0:T(128)} %width_in.1, ...), custom_call_target="tpu_custom_call" | custom-call | tf_op jit(solution)/shard_map/pallas_call | solution.py:613
  47.9 3.7 %shard_map.191 = (f32[192,768]{1,0:T(8,128)}, f32[192,768]{1,0:T(8,128)}, f32[192,768]{1,0:T(8,128)}, f32[384,512]{1,0:T(8,128)}, f32[384,512]{1,0:T(8,128)}, /*index=5*/f32[384,512]{1,0:T(8,128)}) custom-call(f32[192,768]{1,0:T(8,128)} %get-tuple-element.12.refs_0_, f32[192,768]{1,0:T(8,128)} %get-tuple-element.13.refs_1_, ...), custom_call_target="tpu_custom_call" | custom-call | tf_op jit(solution)/shard_map/pallas_call | solution.py:666
